TPU v7x, 32 devices: a whole 2x2x4 slice. The times are simulated.
32 devices in a mesh: seq: 8 (over z, y), chan: 4 (over x, core).
Axes of the slice: x: 2, y: 2, z: 4, core: 2. Of those that a mesh axis runs over, the one named last changes fastest.
Arguments:
- hyena_query: bfloat16 [4096, 2048], P('chan', 'seq'), may hold values from -36 to 36
- hyena_key: bfloat16 [4096, 2048], P('chan', 'seq'), may hold values from -6 to 6
- hyena_value: bfloat16 [4096, 2048], P('chan', 'seq'), may hold values from -6 to 6
- long_filter: float32 [4096, 2048], P(('chan', 'seq')), may hold values from -4 to 4
- skip_weight: float32 [4096], P(('chan', 'seq')), may hold values from 0.5 to 1.5
- stripe_order: int32 [2048], replicated, may hold values from 0 to 2047, as said below
- query_rows: bfloat16 [2048, 4096], P('seq', 'chan'), may hold values from -6 to 6
- key_rows: bfloat16 [2048, 4096], P('seq', 'chan'), may hold values from -6 to 6
- norm_gain: float32 [4096], P('chan'), may hold values from 0.1 to 1.9
Outputs:
- hyena_output: bfloat16 [4096, 2048], P('chan', 'seq')
- attended: bfloat16 [2048, 4096], P('seq', 'chan')
Inputs may be any that keep to these rules, and one draw needn't show every extreme that they name: stripe_order[256 * s + j] = 8 * j + sigma(s) for 0 <= j < 256 and 0 <= s < 8, where sigma is a permutation of 0 to 7.
All inputs are finite; a program needn't handle non-finite values.
Results may differ from a plain program's by a relative error of at most 0.012.
Values may be sent and summed in bfloat16 or wider, within the bound.
A program may use at most 128 MiB of HBM per device.

v0:
```python
import functools
import math

import jax
import jax.numpy as jnp
import ml_dtypes
import numpy as np
from jax import lax
from jax.experimental import pallas as pl
from jax.experimental.pallas import tpu as pltpu
from jax.sharding import PartitionSpec as P

D = 4096
HEAD_DIM = 128
TILES = 4
MESH = pl.DeviceIdType.MESH
PRODUCT, QUERIES, KEYS, GATES, BANDED, ATTENDED, SQUARES = range(7)
TRANSPOSED = (((1,), (1,)), ((), ()))


def high_low(table):
    high = table.astype(ml_dtypes.bfloat16)
    low = (table - high.astype(np.float64)).astype(ml_dtypes.bfloat16)
    return np.stack((high, low))


def odd_tables(stripes, rows):
    frequency = np.arange(rows, dtype=np.float64) + 0.5
    angle = 2.0 * np.pi * frequency[:, None] * np.arange(rows)[None, :] / (2 * rows)
    dense = np.concatenate((np.cos(angle), -np.sin(angle)), axis=0)
    twist = 2.0 * np.pi * frequency[:, None] * np.arange(stripes)[None, :] / (2 * rows * stripes)
    turns = np.zeros((rows, 128), np.float32)
    turns[:, :stripes] = np.cos(twist)
    turns[:, stripes : 2 * stripes] = np.sin(twist)
    return high_low(dense), high_low(dense.T), turns


def small_dft(parts, sign):
    count = len(parts)
    if count == 1:
        return parts
    even = small_dft(parts[0::2], sign)
    odd = small_dft(parts[1::2], sign)
    first, second = [], []
    for k in range(count // 2):
        real, imag = odd[k]
        cos = math.cos(2.0 * math.pi * k / count)
        sin = sign * math.sin(2.0 * math.pi * k / count)
        if k == 0:
            turned = (real, imag)
        elif 4 * k == count:
            turned = (-sign * imag, sign * real)
        else:
            turned = (real * cos - imag * sin, real * sin + imag * cos)
        first.append((even[k][0] + turned[0], even[k][1] + turned[1]))
        second.append((even[k][0] - turned[0], even[k][1] - turned[1]))
    return first + second


def dot(left, right):
    return jnp.dot(left, right, preferred_element_type=jnp.float32)


def split(wide):
    high = wide.astype(jnp.bfloat16)
    return high, (wide - high.astype(jnp.float32)).astype(jnp.bfloat16)


def fused_kernel(
    n,
    chans,
    order_ref,
    hk_ref,
    hv_ref,
    skip_ref,
    gain_ref,
    hq_hbm,
    filter_hbm,
    q_hbm,
    k_hbm,
    forward_hbm,
    inverse_hbm,
    turns_hbm,
    banded_ref,
    attended_ref,
    product_out,
    product_in,
    gate_in,
    q_in,
    k_in,
    filter_ref,
    forward_ref,
    inverse_ref,
    turns_ref,
    upright,
    signal,
    section,
    spectrum,
    back,
    convolved,
    gated,
    gated_out,
    weights,
    totals,
    values,
    result,
    squares,
    squares_chan,
    squares_sum,
    squares_seq,
    bias,
    send_sem,
    recv_sem,
    chan_send,
    chan_recv,
    local_sem,
):
    me = lax.axis_index("seq")
    my_chan = lax.axis_index("chan")
    pencil, rows = product_in.shape[1:]
    tile = rows // TILES
    wide_tile = n * tile

    def peer(offset):
        return lax.rem(me + offset, n)

    def block(ref, index):
        return ref.at[pl.ds(pl.multiple_of(index * pencil, pencil), pencil), :]

    def column(ref, index):
        return ref.at[:, pl.ds(pl.multiple_of(index * pencil, pencil), pencil)]

    def exchange(kind, source, target):
        return [
            pltpu.make_async_remote_copy(
                src_ref=source(peer(offset)),
                dst_ref=target,
                send_sem=send_sem.at[kind, offset],
                recv_sem=recv_sem.at[kind, offset],
                device_id={"seq": peer(offset)},
                device_id_type=MESH,
            )
            for offset in range(1, n)
        ]

    barrier = pltpu.get_barrier_semaphore()
    for offset in range(1, n):
        pl.semaphore_signal(barrier, inc=1, device_id={"seq": peer(offset)}, device_id_type=MESH)
    for offset in range(1, chans):
        other = lax.rem(my_chan + offset, chans)
        pl.semaphore_signal(barrier, inc=1, device_id={"chan": other}, device_id_type=MESH)

    staged = [
        (filter_hbm, filter_ref),
        (forward_hbm, forward_ref),
        (inverse_hbm, inverse_ref),
        (turns_hbm, turns_ref),
        (column(q_hbm, me), q_in.at[me]),
        (column(k_hbm, me), k_in.at[me]),
        (block(hq_hbm, me), gate_in.at[me]),
    ]
    staged = [
        pltpu.make_async_copy(source, target, local_sem.at[index])
        for index, (source, target) in enumerate(staged)
    ]
    for copy in staged:
        copy.start()

    def make_product(index, unused):
        part = pl.ds(pl.multiple_of(index * pencil, pencil), pencil)
        product_out[index] = (
            hk_ref[part, :].astype(jnp.float32) * hv_ref[part, :].astype(jnp.float32)
        ).astype(jnp.bfloat16)
        return unused

    lax.fori_loop(0, n, make_product, 0)
    pl.semaphore_wait(barrier, n - 1 + chans - 1)
    products = exchange(PRODUCT, lambda d: product_out.at[d], product_in.at[me])
    for copy in products:
        copy.start()
    product_in[me] = product_out[me]

    for copy in staged[:4]:
        copy.wait()

    def turned_sections(part):
        cos = turns_ref[part, :]
        parts = []
        for t in range(n):
            real = section[part, t * pencil : (t + 1) * pencil]
            below = pl.ds(pl.multiple_of(rows + part.start, part.size), part.size)
            imag = section[below, t * pencil : (t + 1) * pencil]
            c, s = cos[:, t : t + 1], cos[:, n + t : n + t + 1]
            parts.append((real * c + imag * s, imag * c - real * s))
        return small_dft(parts, -1.0)

    step = 16

    def filter_spectrum(index, unused):
        part = pl.ds(pl.multiple_of(index * step, step), step)
        scale = 1.0 / (rows * n)
        for k, (real, imag) in enumerate(turned_sections(part)):
            spectrum[0, part, k * pencil : (k + 1) * pencil] = real * scale
            spectrum[1, part, k * pencil : (k + 1) * pencil] = imag * scale
        return unused

    def signal_spectrum(index, unused):
        part = pl.ds(pl.multiple_of(index * step, step), step)
        below = pl.ds(pl.multiple_of(rows + index * step, step), step)
        parts = []
        for k, (real, imag) in enumerate(turned_sections(part)):
            other_real = spectrum[0, part, k * pencil : (k + 1) * pencil]
            other_imag = spectrum[1, part, k * pencil : (k + 1) * pencil]
            parts.append(
                (real * other_real - imag * other_imag, real * other_imag + imag * other_real)
            )
        cos = turns_ref[part, :]
        for t, (real, imag) in enumerate(small_dft(parts, 1.0)):
            c, s = cos[:, t : t + 1], cos[:, n + t : n + t + 1]
            lanes = slice(t * pencil, (t + 1) * pencil)
            for place, value in ((part, real * c - imag * s), (below, real * s + imag * c)):
                high, low = split(value)
                back[0, place, lanes] = high
                back[1, place, lanes] = low
        return unused

    for s in range(n):
        upright[s * rows : (s + 1) * rows, :] = filter_ref[:, s * rows : (s + 1) * rows].T
    for t in range(0, n, 2):
        pair = jnp.concatenate(
            [upright[pl.ds(t + u, rows, stride=n), :] for u in range(2)], axis=1
        )
        high, low = split(pair)
        section[:, t * pencil : (t + 2) * pencil] = (
            dot(forward_ref[0], high) + dot(forward_ref[1], high) + dot(forward_ref[0], low)
        )
    lax.fori_loop(0, rows // step, filter_spectrum, 0)

    def place_of(index, count):
        inner = lax.rem(index, tile)
        place = n * inner
        for s in range(n):
            place = place + jnp.where(index // tile == s, order_ref[s * rows], 0)
        return place

    key_place = place_of(lax.broadcasted_iota(jnp.int32, (8, wide_tile), 1), wide_tile)[:1]
    query_place = place_of(lax.broadcasted_iota(jnp.int32, (wide_tile, 128), 0), wide_tile)[:, :1]
    bias[...] = jnp.where(key_place <= query_place, 0.0, -1e30)

    for copy in products:
        copy.wait()

    queries = exchange(QUERIES, lambda d: column(q_hbm, d), q_in.at[me])
    keys = exchange(KEYS, lambda d: column(k_hbm, d), k_in.at[me])
    gates = exchange(GATES, lambda d: block(hq_hbm, d), gate_in.at[me])
    for copy in queries + keys + gates:
        copy.start()

    def stand_up(source):
        for s in range(n):
            upright[s * rows : (s + 1) * rows, :] = source[s].astype(jnp.float32).T

    stand_up(product_in)
    for t in range(0, n, 2):
        pair = [upright[pl.ds(t + u, rows, stride=n), :] for u in range(2)]
        signal[t] = pair[0]
        signal[t + 1] = pair[1]
        exact = jnp.concatenate(pair, axis=1).astype(jnp.bfloat16)
        section[:, t * pencil : (t + 2) * pencil] = dot(forward_ref[0], exact) + dot(
            forward_ref[1], exact
        )
    lax.fori_loop(0, rows // step, signal_spectrum, 0)
    for t in range(0, n, 2):
        lanes = slice(t * pencil, (t + 2) * pencil)
        high, low = back[0, :, lanes], back[1, :, lanes]
        pair = dot(inverse_ref[0], high) + dot(inverse_ref[1], high) + dot(inverse_ref[0], low)
        for u in range(2):
            convolved[t + u] = (
                pair[:, u * pencil : (u + 1) * pencil] + skip_ref[...] * signal[t + u]
            )

    for copy in queries + keys:
        copy.wait()
    for copy in staged[4:]:
        copy.wait()

    factor = math.log2(math.e) / math.sqrt(HEAD_DIM)
    half = n // 2
    for jt in range(TILES):
        for h in range(2):
            mine = slice(h * half * tile, (h + 1) * half * tile)
            query = q_in[h * half : (h + 1) * half, jt * tile : (jt + 1) * tile, :]
            query = query.reshape(half * tile, pencil)
            scores = []
            for kt in range(jt + 1):
                key = k_in[:, kt * tile : (kt + 1) * tile, :].reshape(wide_tile, pencil)
                score = lax.dot_general(
                    query, key, TRANSPOSED, preferred_element_type=jnp.float32
                )
                scores.append(score + bias[mine, :] if kt == jt else score)
            top = functools.reduce(jnp.maximum, [jnp.max(s, axis=1, keepdims=True) for s in scores])
            total = jnp.zeros((half * tile, 1), jnp.float32)
            for kt, score in enumerate(scores):
                weight = jnp.exp2((score - top) * factor)
                total = total + jnp.sum(weight, axis=1, keepdims=True)
                weights[jt, mine, kt * wide_tile : (kt + 1) * wide_tile] = weight.astype(
                    jnp.bfloat16
                )
            totals[jt, mine, :] = jnp.broadcast_to(total, (half * tile, pencil))

    for copy in gates:
        copy.wait()
    stand_up(gate_in)
    for t in range(n):
        gated[t] = (upright[pl.ds(t, rows, stride=n), :] * convolved[t]).astype(jnp.bfloat16)

    banded = exchange(BANDED, lambda d: gated_out.at[d], block(banded_ref, me))
    ones = jnp.ones((8, pencil), jnp.float32)
    for offset in list(range(1, n)) + [0]:
        to = peer(offset)
        mine = gated[order_ref[to * rows]].astype(jnp.float32)
        gated_out[to] = mine.T.astype(jnp.bfloat16)
        if offset:
            banded[offset - 1].start()
    own_banded = pltpu.make_async_copy(gated_out.at[me], block(banded_ref, me), local_sem.at[0])
    own_banded.start()
    for s in range(n):
        mine = gated[order_ref[s * rows]].astype(jnp.float32)
        values[s] = mine.astype(jnp.bfloat16)
        squares[s : s + 1, :] = lax.dot_general(
            ones,
            mine * mine,
            TRANSPOSED,
            precision=lax.Precision.HIGHEST,
            preferred_element_type=jnp.float32,
        )[:1]
    across = [
        pltpu.make_async_remote_copy(
            src_ref=squares,
            dst_ref=squares_chan.at[offset],
            send_sem=chan_send.at[offset],
            recv_sem=chan_recv.at[offset],
            device_id={"chan": lax.rem(my_chan + offset, chans)},
            device_id_type=MESH,
        )
        for offset in range(1, chans)
    ]
    for copy in across:
        copy.start()
    for copy in across:
        copy.wait()
    squares_sum[...] = functools.reduce(
        jnp.add, [squares[...]] + [squares_chan[offset] for offset in range(1, chans)]
    )
    along = exchange(SQUARES, lambda d: squares_sum, squares_seq.at[me])
    for copy in along:
        copy.start()
    squares_seq[me] = squares_sum[...]
    for copy in along:
        copy.wait()
    inverse_rms = lax.rsqrt(
        functools.reduce(jnp.add, [squares_seq[s] for s in range(n)]) / D + 1e-05
    )
    gain = gain_ref[pl.ds(me, 1), :]
    for s in range(n):
        scale = jnp.broadcast_to(inverse_rms[s : s + 1, :], (pencil, rows)).T
        values[s] = (values[s].astype(jnp.float32) * scale * gain).astype(jnp.bfloat16)

    for h in range(2):
        mine = slice(h * half * tile, (h + 1) * half * tile)
        for jt in range(TILES):
            total = jnp.zeros((half * tile, pencil), jnp.float32)
            for kt in range(jt + 1):
                value = values[:, kt * tile : (kt + 1) * tile, :].reshape(wide_tile, pencil)
                total = total + dot(weights[jt, mine, kt * wide_tile : (kt + 1) * wide_tile], value)
            part = (total / totals[jt, mine, :]).astype(jnp.bfloat16)
            result[h * half : (h + 1) * half, jt * tile : (jt + 1) * tile, :] = part.reshape(
                half, tile, pencil
            )
    attended = exchange(ATTENDED, lambda d: result.at[d], column(attended_ref, me))
    for copy in attended:
        copy.start()
    own_attended = pltpu.make_async_copy(result.at[me], column(attended_ref, me), local_sem.at[1])
    own_attended.start()
    for copy in banded + attended + [own_banded, own_attended]:
        copy.wait()


def fused(
    hyena_query,
    hyena_key,
    hyena_value,
    long_filter,
    skip_weight,
    stripe_order,
    query_rows,
    key_rows,
    norm_gain,
):
    n = lax.axis_size("seq")
    chans = lax.axis_size("chan")
    channels, rows = hyena_query.shape
    pencil = long_filter.shape[0]
    forward_table, inverse_table, turns = odd_tables(n, rows)
    vmem = pl.BlockSpec(memory_space=pltpu.VMEM)
    anywhere = pl.BlockSpec(memory_space=pl.ANY)
    bf16, f32 = jnp.bfloat16, jnp.float32
    wide = n * pencil
    tile = rows // TILES
    return pl.pallas_call(
        functools.partial(fused_kernel, n, chans),
        out_shape=(
            jax.ShapeDtypeStruct((channels, rows), bf16),
            jax.ShapeDtypeStruct((rows, channels), bf16),
        ),
        in_specs=[pl.BlockSpec(memory_space=pltpu.SMEM)] + [vmem] * 4 + [anywhere] * 7,
        out_specs=(anywhere, anywhere),
        scratch_shapes=[
            pltpu.VMEM((n, pencil, rows), bf16),
            pltpu.VMEM((n, pencil, rows), bf16),
            pltpu.VMEM((n, pencil, rows), bf16),
            pltpu.VMEM((n, rows, pencil), bf16),
            pltpu.VMEM((n, rows, pencil), bf16),
            pltpu.VMEM(long_filter.shape, f32),
            pltpu.VMEM(forward_table.shape, bf16),
            pltpu.VMEM(inverse_table.shape, bf16),
            pltpu.VMEM(turns.shape, f32),
            pltpu.VMEM((n * rows, pencil), f32),
            pltpu.VMEM((n, rows, pencil), f32),
            pltpu.VMEM((2 * rows, wide), f32),
            pltpu.VMEM((2, rows, wide), f32),
            pltpu.VMEM((2, 2 * rows, wide), bf16),
            pltpu.VMEM((n, rows, pencil), f32),
            pltpu.VMEM((n, rows, pencil), bf16),
            pltpu.VMEM((n, pencil, rows), bf16),
            pltpu.VMEM((TILES, n * tile, n * rows), bf16),
            pltpu.VMEM((TILES, n * tile, pencil), f32),
            pltpu.VMEM((n, rows, pencil), bf16),
            pltpu.VMEM((n, rows, pencil), bf16),
            pltpu.VMEM((n, rows), f32),
            pltpu.VMEM((chans, n, rows), f32),
            pltpu.VMEM((n, rows), f32),
            pltpu.VMEM((n, n, rows), f32),
            pltpu.VMEM((n * tile, n * tile), f32),
            pltpu.SemaphoreType.DMA((7, n)),
            pltpu.SemaphoreType.DMA((7, n)),
            pltpu.SemaphoreType.DMA((chans,)),
            pltpu.SemaphoreType.DMA((chans,)),
            pltpu.SemaphoreType.DMA((7,)),
        ],
        compiler_params=pltpu.CompilerParams(
            collective_id=0, has_side_effects=True, vmem_limit_bytes=56 * 1024 * 1024
        ),
    )(
        stripe_order,
        hyena_key,
        hyena_value,
        skip_weight.reshape(1, pencil),
        norm_gain.reshape(n, pencil),
        hyena_query,
        long_filter,
        query_rows,
        key_rows,
        jnp.asarray(forward_table),
        jnp.asarray(inverse_table),
        jnp.asarray(turns),
    )


def passed_along(block, axis, distance):
    devices = range(lax.axis_size(axis))
    route = [((i - distance) % len(devices), i) for i in devices]
    return lax.ppermute(block, axis, route)


def angle_table(first, second, modulus):
    left = jnp.arange(first, dtype=jnp.int32)[:, None]
    right = jnp.arange(second, dtype=jnp.int32)[None, :]
    theta = 2.0 * math.pi / modulus * (left * right % modulus).astype(jnp.float32)
    return (jnp.cos(theta), jnp.sin(theta))


def transform_tables(length):
    outer = 2 * length // 128
    first_cos, first_sin = angle_table(outer, outer // 2, outer)
    twist_cos, twist_sin = angle_table(outer, 128, 2 * length)
    inner_cos, inner_sin = angle_table(128, 128, 128)
    return (first_cos, first_sin, twist_cos, twist_sin, inner_cos, inner_sin)


def contract(form, left, right):
    return jnp.einsum(form, left, right, precision=lax.Precision.HIGHEST)


def forward(signal, tables):
    first_cos, first_sin, twist_cos, twist_sin, inner_cos, inner_sin = tables
    section_real = contract("kt,cts->cks", first_cos, signal)
    section_imag = -contract("kt,cts->cks", first_sin, signal)
    turned_real = section_real * twist_cos + section_imag * twist_sin
    turned_imag = section_imag * twist_cos - section_real * twist_sin
    out_real = contract("cks,sm->ckm", turned_real, inner_cos) + contract(
        "cks,sm->ckm", turned_imag, inner_sin
    )
    out_imag = contract("cks,sm->ckm", turned_imag, inner_cos) - contract(
        "cks,sm->ckm", turned_real, inner_sin
    )
    return (out_real, out_imag)


def inverse(spectrum_real, spectrum_imag, tables):
    first_cos, first_sin, twist_cos, twist_sin, inner_cos, inner_sin = tables
    back_real = contract("ckm,sm->cks", spectrum_real, inner_cos) - contract(
        "ckm,sm->cks", spectrum_imag, inner_sin
    )
    back_imag = contract("ckm,sm->cks", spectrum_real, inner_sin) + contract(
        "ckm,sm->cks", spectrum_imag, inner_cos
    )
    turned_real = back_real * twist_cos - back_imag * twist_sin
    turned_imag = back_real * twist_sin + back_imag * twist_cos
    signal = contract("kt,cks->cts", first_cos, turned_real) - contract(
        "kt,cks->cts", first_sin, turned_imag
    )
    return signal * (1.0 / (first_cos.shape[0] * 128))


def convolve(signal, filter_parts, tables):
    pencil, length = signal.shape
    widened = signal.astype(jnp.float32).reshape(pencil, length // 128, 128)
    signal_real, signal_imag = forward(widened, tables)
    filter_real, filter_imag = filter_parts
    product_real = signal_real * filter_real - signal_imag * filter_imag
    product_imag = signal_real * filter_imag + signal_imag * filter_real
    return inverse(product_real, product_imag, tables).reshape(pencil, length)


def fold_keys(carry, queries, own_places, key_piece, value_piece, places, scale):
    count = key_piece.shape[0]
    heads = queries.shape[1]
    depth = queries.shape[2]
    block = math.gcd(count, 512)
    place_blocks = places.reshape(count // block, block)
    key_blocks = key_piece.reshape(count // block, block, heads, depth)
    value_blocks = value_piece.reshape(count // block, block, heads, depth)

    def one_block(state, inputs):
        running, totals, sums = state
        key_block, value_block, key_places = inputs
        scores = (
            jnp.einsum("qhd,khd->hqk", queries, key_block, preferred_element_type=jnp.float32)
            * scale
        )
        allowed = key_places[None, None, :] <= own_places[None, :, None]
        scores = jnp.where(allowed, scores, -1e30)
        highest = jnp.maximum(running, jnp.max(scores, axis=2))
        weights = jnp.where(allowed, jnp.exp(scores - highest[:, :, None]), 0.0)
        factor = jnp.exp(running - highest)
        totals = totals * factor + jnp.sum(weights, axis=2)
        update = jnp.einsum(
            "hqk,khd->hqd",
            weights.astype(jnp.bfloat16),
            value_block,
            preferred_element_type=jnp.float32,
        )
        sums = sums * factor[:, :, None] + update
        return ((highest, totals, sums), None)

    carry, unused = lax.scan(one_block, carry, (key_blocks, value_blocks, place_blocks))
    return carry


def general(
    hyena_query,
    hyena_key,
    hyena_value,
    long_filter,
    skip_weight,
    stripe_order,
    query_rows,
    key_rows,
    norm_gain,
):
    stripes = lax.axis_size("seq")
    channels, rows = hyena_query.shape
    pencil, length = long_filter.shape
    sigma = stripe_order.reshape(stripes, rows)[:, 0]
    product = (hyena_key.astype(jnp.float32) * hyena_value.astype(jnp.float32)).astype(jnp.bfloat16)
    tables = transform_tables(length)
    filter_parts = forward(long_filter.reshape(pencil, length // 128, 128), tables)
    spread = lax.all_to_all(product, "seq", split_axis=0, concat_axis=1, tiled=True)
    summed = convolve(spread, filter_parts, tables) + skip_weight[:, None] * spread.astype(
        jnp.float32
    )
    returned = lax.all_to_all(
        summed.astype(jnp.bfloat16), "seq", split_axis=1, concat_axis=0, tiled=True
    ).astype(summed.dtype)
    gated = (hyena_query.astype(jnp.float32) * returned).astype(jnp.bfloat16)
    per_stripe = rows // stripes
    columns = stripes * jnp.arange(per_stripe, dtype=jnp.int32)[None, :] + sigma[:, None]
    arranged = jnp.take(gated, columns.reshape(rows), axis=1).reshape(channels, stripes, per_stripe)
    banded = lax.all_to_all(arranged, "seq", split_axis=1, concat_axis=2, tiled=True).reshape(
        channels, rows
    )
    output_wide = banded.astype(jnp.float32)
    squares = lax.psum(jnp.sum(output_wide * output_wide, axis=0), "chan")
    inverse_rms = lax.rsqrt(squares / D + 1e-05)
    normed = (output_wide * inverse_rms[None, :] * norm_gain[:, None]).astype(jnp.bfloat16)
    value_rows = normed.T
    local_heads = channels // HEAD_DIM
    scale = 1.0 / math.sqrt(HEAD_DIM)
    seq_index = lax.axis_index("seq")
    own_head = seq_index % local_heads
    group_index = seq_index // local_heads
    group_count = stripes // local_heads
    span = local_heads * rows
    stacked_local = jnp.stack((query_rows, key_rows, value_rows)).reshape(
        3, rows, local_heads, HEAD_DIM
    )
    collected = [lax.dynamic_index_in_dim(stacked_local, own_head, 2, keepdims=False)]
    for offset in range(1, local_heads):
        payload = lax.dynamic_index_in_dim(
            stacked_local, (own_head + offset) % local_heads, 2, keepdims=False
        )
        from_below = passed_along(payload, "seq", offset)
        from_above = passed_along(payload, "seq", offset - local_heads)
        collected.append(jnp.where(own_head >= offset, from_below, from_above))
    ordering = (own_head - jnp.arange(local_heads, dtype=jnp.int32)) % local_heads
    sources = jnp.take(jnp.stack(collected), ordering, axis=0)
    combined = sources.transpose(1, 0, 2, 3).reshape(3, span, HEAD_DIM)
    group_places = lax.dynamic_slice_in_dim(stripe_order, group_index * span, span)
    group_queries = combined[0].reshape(span, 1, HEAD_DIM)

    def visit(state, kv_pair, source):
        places = lax.dynamic_slice_in_dim(stripe_order, source * span, span)
        return fold_keys(
            state,
            group_queries,
            group_places,
            kv_pair[0].reshape(span, 1, HEAD_DIM),
            kv_pair[1].reshape(span, 1, HEAD_DIM),
            places,
            scale,
        )

    initial_group = (
        jnp.full((1, span), -1e30, jnp.float32),
        jnp.zeros((1, span), jnp.float32),
        jnp.zeros((1, span, HEAD_DIM), jnp.float32),
    )

    def cycle_turn(turn, loop_state):
        state, kv_pair = loop_state
        state = visit(state, kv_pair, (group_index - turn) % group_count)
        kv_pair = passed_along(kv_pair, "seq", local_heads)
        return (state, kv_pair)

    state, kv_pair = lax.fori_loop(0, group_count - 1, cycle_turn, (initial_group, combined[1:]))
    running, totals, sums = visit(state, kv_pair, (group_index - (group_count - 1)) % group_count)
    result = (sums[0] / totals[0][:, None]).astype(jnp.bfloat16)
    pieces = result.reshape(local_heads, rows, HEAD_DIM)
    returned_heads = [lax.dynamic_index_in_dim(pieces, own_head, 0, keepdims=False)]
    for offset in range(1, local_heads):
        payload = lax.dynamic_index_in_dim(
            pieces, (own_head + offset) % local_heads, 0, keepdims=False
        )
        back_below = passed_along(payload, "seq", offset)
        back_above = passed_along(payload, "seq", offset - local_heads)
        returned_heads.append(jnp.where(own_head >= offset, back_below, back_above))
    by_head = jnp.take(jnp.stack(returned_heads), ordering, axis=0)
    attended = by_head.transpose(1, 0, 2).reshape(rows, channels)
    return (banded, attended)


def local(*arrays):
    pencil = arrays[3].shape[0]
    rows = arrays[0].shape[1]
    stripes = lax.axis_size("seq")
    even = stripes % 2 == 0 and stripes & (stripes - 1) == 0 and 2 * stripes <= HEAD_DIM
    one_head = pencil == HEAD_DIM and even and rows % (16 * TILES) == 0
    return fused(*arrays) if one_head else general(*arrays)


def solution(mesh):
    placed = (
        P("chan", "seq"),
        P("chan", "seq"),
        P("chan", "seq"),
        P(("chan", "seq"), None),
        P(("chan", "seq")),
        P(),
        P("seq", "chan"),
        P("seq", "chan"),
        P("chan"),
    )
    return jax.shard_map(
        local,
        mesh=mesh,
        in_specs=placed,
        out_specs=(P("chan", "seq"), P("seq", "chan")),
        check_vma=False,
    )
```

profile of v0, /device:TPU:14, one launch (start us, length us, event | category | flops | bytes accessed | tf_op | source)
XLA Modules:
  0.0 86.6 jit_solution(18250482086694166846)
XLA Ops:
  0.6 83.2 %shard_map.131 = (bf16[1024,256]{1,0:T(8,128)(2,1)}, bf16[256,1024]{1,0:T(8,128)(2,1)}) custom-call(s32[2048]{0:T(1024)} %order_ref.1, bf16[1024,256]{1,0:T(8,128)(2,1)} %hk_ref.1, bf16[1024,256]{1,0:T(8,128)(2,1)} %hv_ref.1, f32[1,128]{1,0:T(1,128)} %bitcast.3, f32[8,128]{1,0:T(8,128)} %bitcast.2, bf16[1024,256]{1,0:T(8,128)(2,1)} %hq_hbm.1, ...), custom_call_target="tpu_custom_call" | custom-call | tf_op jit(solution)/shard_map/pallas_call | solution.py:410
  83.9 0.0 copy-start
  83.9 1.9 %copy.16 = bf16[1024,256]{1,0:T(8,128)(2,1)} copy(bf16[1024,256]{1,0:T(8,128)(2,1)} %get-tuple-element.4) | data formatting | bytes 1048576
  85.8 0.0 copy-done
  85.8 0.8 copy.17
Async XLA Ops:
  83.9 1.9 %copy-start = (bf16[256,1024]{1,0:T(8,128)(2,1)S(1)}, bf16[256,1024]{1,0:T(8,128)(2,1)}, u32[]{:S(2)}) copy-start(bf16[256,1024]{1,0:T(8,128)(2,1)} %get-tuple-element.5) | copy-start | bytes 1572868
where the time goes:
time: 86.8 us; the launch traced here: 86.6 us
  Pallas kernels  83.2 us (96%)
  local copies, waits for them, and re-layouts  2.72 us (3%)
    pallas_call x1, Pallas kernels, fused(): pl.pallas_call(functools.partial(fused_kernel, n, chans), out_shape=(jax....  83.2 us
    unnamed x4, local copies, waits for them, and re-layouts  2.72 us

commit v1 on v0

--- a/solution.py
+++ b/solution.py
@@ -100,8 +100,6 @@
     convolved,
     gated,
     gated_out,
-    weights,
-    totals,
     values,
     result,
     squares,
@@ -176,7 +174,10 @@
     lax.fori_loop(0, n, make_product, 0)
     pl.semaphore_wait(barrier, n - 1 + chans - 1)
     products = exchange(PRODUCT, lambda d: product_out.at[d], product_in.at[me])
-    for copy in products:
+    queries = exchange(QUERIES, lambda d: column(q_hbm, d), q_in.at[me])
+    keys = exchange(KEYS, lambda d: column(k_hbm, d), k_in.at[me])
+    gates = exchange(GATES, lambda d: block(hq_hbm, d), gate_in.at[me])
+    for copy in products + gates:
         copy.start()
     product_in[me] = product_out[me]
 
@@ -235,6 +236,8 @@
             dot(forward_ref[0], high) + dot(forward_ref[1], high) + dot(forward_ref[0], low)
         )
     lax.fori_loop(0, rows // step, filter_spectrum, 0)
+    for copy in queries:
+        copy.start()
 
     def place_of(index, count):
         inner = lax.rem(index, tile)
@@ -250,10 +253,7 @@
     for copy in products:
         copy.wait()
 
-    queries = exchange(QUERIES, lambda d: column(q_hbm, d), q_in.at[me])
-    keys = exchange(KEYS, lambda d: column(k_hbm, d), k_in.at[me])
-    gates = exchange(GATES, lambda d: block(hq_hbm, d), gate_in.at[me])
-    for copy in queries + keys + gates:
+    for copy in keys:
         copy.start()
 
     def stand_up(source):
@@ -279,35 +279,8 @@
                 pair[:, u * pencil : (u + 1) * pencil] + skip_ref[...] * signal[t + u]
             )
 
-    for copy in queries + keys:
-        copy.wait()
     for copy in staged[4:]:
         copy.wait()
-
-    factor = math.log2(math.e) / math.sqrt(HEAD_DIM)
-    half = n // 2
-    for jt in range(TILES):
-        for h in range(2):
-            mine = slice(h * half * tile, (h + 1) * half * tile)
-            query = q_in[h * half : (h + 1) * half, jt * tile : (jt + 1) * tile, :]
-            query = query.reshape(half * tile, pencil)
-            scores = []
-            for kt in range(jt + 1):
-                key = k_in[:, kt * tile : (kt + 1) * tile, :].reshape(wide_tile, pencil)
-                score = lax.dot_general(
-                    query, key, TRANSPOSED, preferred_element_type=jnp.float32
-                )
-                scores.append(score + bias[mine, :] if kt == jt else score)
-            top = functools.reduce(jnp.maximum, [jnp.max(s, axis=1, keepdims=True) for s in scores])
-            total = jnp.zeros((half * tile, 1), jnp.float32)
-            for kt, score in enumerate(scores):
-                weight = jnp.exp2((score - top) * factor)
-                total = total + jnp.sum(weight, axis=1, keepdims=True)
-                weights[jt, mine, kt * wide_tile : (kt + 1) * wide_tile] = weight.astype(
-                    jnp.bfloat16
-                )
-            totals[jt, mine, :] = jnp.broadcast_to(total, (half * tile, pencil))
-
     for copy in gates:
         copy.wait()
     stand_up(gate_in)
@@ -320,10 +293,6 @@
         to = peer(offset)
         mine = gated[order_ref[to * rows]].astype(jnp.float32)
         gated_out[to] = mine.T.astype(jnp.bfloat16)
-        if offset:
-            banded[offset - 1].start()
-    own_banded = pltpu.make_async_copy(gated_out.at[me], block(banded_ref, me), local_sem.at[0])
-    own_banded.start()
     for s in range(n):
         mine = gated[order_ref[s * rows]].astype(jnp.float32)
         values[s] = mine.astype(jnp.bfloat16)
@@ -366,24 +335,88 @@
         scale = jnp.broadcast_to(inverse_rms[s : s + 1, :], (pencil, rows)).T
         values[s] = (values[s].astype(jnp.float32) * scale * gain).astype(jnp.bfloat16)
 
-    for h in range(2):
-        mine = slice(h * half * tile, (h + 1) * half * tile)
+    for copy in keys:
+        copy.wait_send()
+    for copy in banded:
+        copy.start()
+    own_banded = pltpu.make_async_copy(gated_out.at[me], block(banded_ref, me), local_sem.at[0])
+    own_banded.start()
+    for copy in queries:
+        copy.wait()
+    for copy in keys:
+        copy.wait_recv()
+
+    factor = math.log2(math.e) / math.sqrt(HEAD_DIM)
+    half = n // 2
+    height = half * tile
+    attended = exchange(ATTENDED, lambda d: result.at[d], column(attended_ref, me))
+
+    def attend_half(turn, unused):
+        h = lax.rem(1 - me // half + turn, 2)
+        first = pl.multiple_of(h * half, half)
         for jt in range(TILES):
-            total = jnp.zeros((half * tile, pencil), jnp.float32)
+            query = q_in[pl.ds(first, half), jt * tile : (jt + 1) * tile, :]
+            query = query.reshape(height, pencil)
+            scores = []
             for kt in range(jt + 1):
+                key = k_in[:, kt * tile : (kt + 1) * tile, :].reshape(wide_tile, pencil)
+                score = lax.dot_general(
+                    query, key, TRANSPOSED, preferred_element_type=jnp.float32
+                )
+                if kt == jt:
+                    score = score + bias[pl.ds(pl.multiple_of(h * height, height), height), :]
+                scores.append(score)
+            top = functools.reduce(jnp.maximum, [jnp.max(s, axis=1, keepdims=True) for s in scores])
+            total = jnp.zeros((height, 1), jnp.float32)
+            summed = jnp.zeros((height, pencil), jnp.float32)
+            for kt, score in enumerate(scores):
+                weight = jnp.exp2((score - top) * factor)
+                total = total + jnp.sum(weight, axis=1, keepdims=True)
                 value = values[:, kt * tile : (kt + 1) * tile, :].reshape(wide_tile, pencil)
-                total = total + dot(weights[jt, mine, kt * wide_tile : (kt + 1) * wide_tile], value)
-            part = (total / totals[jt, mine, :]).astype(jnp.bfloat16)
-            result[h * half : (h + 1) * half, jt * tile : (jt + 1) * tile, :] = part.reshape(
+                summed = summed + dot(weight.astype(jnp.bfloat16), value)
+            part = (summed / total).astype(jnp.bfloat16)
+            result[pl.ds(first, half), jt * tile : (jt + 1) * tile, :] = part.reshape(
                 half, tile, pencil
             )
-    attended = exchange(ATTENDED, lambda d: result.at[d], column(attended_ref, me))
-    for copy in attended:
-        copy.start()
+        for offset in range(1, n):
+
+            @pl.when(peer(offset) // half == h)
+            def send():
+                attended[offset - 1].start()
+
+        return unused
+
+    lax.fori_loop(0, 2, attend_half, 0)
     own_attended = pltpu.make_async_copy(result.at[me], column(attended_ref, me), local_sem.at[1])
     own_attended.start()
     for copy in banded + attended + [own_banded, own_attended]:
         copy.wait()
+
+
+def settle_kernel(banded_ref, attended_ref, banded_out, attended_out, sems):
+    copies = []
+    for source, target in ((banded_ref, banded_out), (attended_ref, attended_out)):
+        part = source.shape[0] // 4
+        for index in range(4):
+            rows = pl.ds(index * part, part)
+            copies.append(
+                pltpu.make_async_copy(source.at[rows], target.at[rows], sems.at[len(copies)])
+            )
+    for copy in copies:
+        copy.start()
+    for copy in copies:
+        copy.wait()
+
+
+def settled(*arrays):
+    anywhere = pl.BlockSpec(memory_space=pl.ANY)
+    return pl.pallas_call(
+        settle_kernel,
+        out_shape=tuple(jax.ShapeDtypeStruct(a.shape, a.dtype) for a in arrays),
+        in_specs=[anywhere] * 2,
+        out_specs=(anywhere, anywhere),
+        scratch_shapes=[pltpu.SemaphoreType.DMA((8,))],
+    )(*arrays)
 
 
 def fused(
@@ -407,7 +440,7 @@
     bf16, f32 = jnp.bfloat16, jnp.float32
     wide = n * pencil
     tile = rows // TILES
-    return pl.pallas_call(
+    outputs = pl.pallas_call(
         functools.partial(fused_kernel, n, chans),
         out_shape=(
             jax.ShapeDtypeStruct((channels, rows), bf16),
@@ -433,8 +466,6 @@
             pltpu.VMEM((n, rows, pencil), f32),
             pltpu.VMEM((n, rows, pencil), bf16),
             pltpu.VMEM((n, pencil, rows), bf16),
-            pltpu.VMEM((TILES, n * tile, n * rows), bf16),
-            pltpu.VMEM((TILES, n * tile, pencil), f32),
             pltpu.VMEM((n, rows, pencil), bf16),
             pltpu.VMEM((n, rows, pencil), bf16),
             pltpu.VMEM((n, rows), f32),
@@ -465,6 +496,7 @@
         jnp.asarray(inverse_table),
         jnp.asarray(turns),
     )
+    return settled(*outputs)
 
 
 def passed_along(block, axis, distance):

time: 86.8 us -> 111 us (1.28)
  the two profiles are of different devices: /device:TPU:14 before, /device:TPU:0 now
where the time goes in v1:
time: 111 us
  Pallas kernels  110 us (99%)
    pallas_call x1, Pallas kernels, fused(): pl.pallas_call(functools.partial(fused_kernel, n, chans), out_shape=(jax....  77.4 us
    pallas_call x1, Pallas kernels, settled(): pl.pallas_call(settle_kernel, out_shape=tuple((jax.ShapeDtypeStruct(a.sha...  32.9 us

profile of v1, /device:TPU:0, one launch (start us, length us, event | category | flops | bytes accessed | tf_op | source)
XLA Modules:
  0.0 111.0 jit_solution(2986686452418049350)
XLA Ops:
  0.6 77.4 %shard_map.131 = (bf16[1024,256]{1,0:T(8,128)(2,1)}, bf16[256,1024]{1,0:T(8,128)(2,1)}) custom-call(s32[2048]{0:T(1024)} %order_ref.1, bf16[1024,256]{1,0:T(8,128)(2,1)} %hk_ref.1, bf16[1024,256]{1,0:T(8,128)(2,1)} %hv_ref.1, f32[1,128]{1,0:T(1,128)} %bitcast.3, f32[8,128]{1,0:T(8,128)} %bitcast.2, bf16[1024,256]{1,0:T(8,128)(2,1)} %hq_hbm.1, ...), custom_call_target="tpu_custom_call" | custom-call | tf_op jit(solution)/shard_map/pallas_call | solution.py:443
  78.1 32.9 %shard_map.132 = (bf16[1024,256]{1,0:T(8,128)(2,1)}, bf16[256,1024]{1,0:T(8,128)(2,1)}) custom-call(bf16[1024,256]{1,0:T(8,128)(2,1)} %get-tuple-element.4.banded_ref, bf16[256,1024]{1,0:T(8,128)(2,1)} %get-tuple-element.5.attended_ref), custom_call_target="tpu_custom_call" | custom-call | tf_op jit(solution)/shard_map/pallas_call | solution.py:413

commit v2 on v1

--- a/solution.py
+++ b/solution.py
@@ -83,6 +83,9 @@
     turns_hbm,
     banded_ref,
     attended_ref,
+    gate_all,
+    q_all,
+    k_all,
     product_out,
     product_in,
     gate_in,
@@ -153,9 +156,9 @@
         (forward_hbm, forward_ref),
         (inverse_hbm, inverse_ref),
         (turns_hbm, turns_ref),
-        (column(q_hbm, me), q_in.at[me]),
-        (column(k_hbm, me), k_in.at[me]),
-        (block(hq_hbm, me), gate_in.at[me]),
+        (hq_hbm, gate_all),
+        (q_hbm, q_all),
+        (k_hbm, k_all),
     ]
     staged = [
         pltpu.make_async_copy(source, target, local_sem.at[index])
@@ -173,16 +176,20 @@
 
     lax.fori_loop(0, n, make_product, 0)
     pl.semaphore_wait(barrier, n - 1 + chans - 1)
+    staged[4].wait()
     products = exchange(PRODUCT, lambda d: product_out.at[d], product_in.at[me])
-    queries = exchange(QUERIES, lambda d: column(q_hbm, d), q_in.at[me])
-    keys = exchange(KEYS, lambda d: column(k_hbm, d), k_in.at[me])
-    gates = exchange(GATES, lambda d: block(hq_hbm, d), gate_in.at[me])
+    queries = exchange(QUERIES, lambda d: column(q_all, d), q_in.at[me])
+    keys = exchange(KEYS, lambda d: column(k_all, d), k_in.at[me])
+    gates = exchange(GATES, lambda d: block(gate_all, d), gate_in.at[me])
     for copy in products + gates:
         copy.start()
     product_in[me] = product_out[me]
-
-    for copy in staged[:4]:
+    gate_in[me] = block(gate_all, me)[...]
+
+    for copy in staged[:4] + staged[5:]:
         copy.wait()
+    q_in[me] = column(q_all, me)[...]
+    k_in[me] = column(k_all, me)[...]
 
     def turned_sections(part):
         cos = turns_ref[part, :]
@@ -279,8 +286,6 @@
                 pair[:, u * pencil : (u + 1) * pencil] + skip_ref[...] * signal[t + u]
             )
 
-    for copy in staged[4:]:
-        copy.wait()
     for copy in gates:
         copy.wait()
     stand_up(gate_in)
@@ -339,8 +344,7 @@
         copy.wait_send()
     for copy in banded:
         copy.start()
-    own_banded = pltpu.make_async_copy(gated_out.at[me], block(banded_ref, me), local_sem.at[0])
-    own_banded.start()
+    block(banded_ref, me)[...] = gated_out[me]
     for copy in queries:
         copy.wait()
     for copy in keys:
@@ -387,35 +391,26 @@
         return unused
 
     lax.fori_loop(0, 2, attend_half, 0)
-    own_attended = pltpu.make_async_copy(result.at[me], column(attended_ref, me), local_sem.at[1])
-    own_attended.start()
-    for copy in banded + attended + [own_banded, own_attended]:
+    column(attended_ref, me)[...] = result[me]
+    for copy in banded + attended:
         copy.wait()
 
 
-def settle_kernel(banded_ref, attended_ref, banded_out, attended_out, sems):
-    copies = []
-    for source, target in ((banded_ref, banded_out), (attended_ref, attended_out)):
-        part = source.shape[0] // 4
-        for index in range(4):
-            rows = pl.ds(index * part, part)
-            copies.append(
-                pltpu.make_async_copy(source.at[rows], target.at[rows], sems.at[len(copies)])
-            )
-    for copy in copies:
-        copy.start()
-    for copy in copies:
-        copy.wait()
+def settle_kernel(banded_ref, attended_ref, banded_out, attended_out):
+    banded_out[...] = banded_ref[...]
+    attended_out[...] = attended_ref[...]
 
 
 def settled(*arrays):
-    anywhere = pl.BlockSpec(memory_space=pl.ANY)
+    specs = [
+        pl.BlockSpec((a.shape[0] // 4, a.shape[1]), lambda index: (index, 0)) for a in arrays
+    ]
     return pl.pallas_call(
         settle_kernel,
         out_shape=tuple(jax.ShapeDtypeStruct(a.shape, a.dtype) for a in arrays),
-        in_specs=[anywhere] * 2,
-        out_specs=(anywhere, anywhere),
-        scratch_shapes=[pltpu.SemaphoreType.DMA((8,))],
+        grid=(4,),
+        in_specs=specs,
+        out_specs=specs,
     )(*arrays)
 
 
@@ -447,8 +442,11 @@
             jax.ShapeDtypeStruct((rows, channels), bf16),
         ),
         in_specs=[pl.BlockSpec(memory_space=pltpu.SMEM)] + [vmem] * 4 + [anywhere] * 7,
-        out_specs=(anywhere, anywhere),
+        out_specs=(vmem, vmem),
         scratch_shapes=[
+            pltpu.VMEM((channels, rows), bf16),
+            pltpu.VMEM((rows, channels), bf16),
+            pltpu.VMEM((rows, channels), bf16),
             pltpu.VMEM((n, pencil, rows), bf16),
             pltpu.VMEM((n, pencil, rows), bf16),
             pltpu.VMEM((n, pencil, rows), bf16),

time: 111 us -> 82.6 us (0.74)
  Pallas kernels: 110 us -> 81.7 us
    pallas_call x1, Pallas kernels: 32.9 us -> 3.41 us  [settled(): pl.pallas_call(settle_kernel, out_shape=tuple((jax.ShapeDtypeStruct(a.sha...]
where the time goes in v2:
time: 82.6 us; the launch traced here: 82.4 us
  Pallas kernels  81.7 us (99%)
    pallas_call x1, Pallas kernels, fused(): pl.pallas_call(functools.partial(fused_kernel, n, chans), out_shape=(jax....  78.3 us
    pallas_call x1, Pallas kernels, settled(): pl.pallas_call(settle_kernel, out_shape=tuple((jax.ShapeDtypeStruct(a.sha...  3.41 us

profile of v2, /device:TPU:0, one launch (start us, length us, event | category | flops | bytes accessed | tf_op | source)
XLA Modules:
  0.0 82.4 jit_solution(2487168815409520152)
XLA Ops:
  0.6 78.3 %shard_map.131 = (bf16[1024,256]{1,0:T(8,128)(2,1)}, bf16[256,1024]{1,0:T(8,128)(2,1)}) custom-call(s32[2048]{0:T(1024)} %order_ref.1, bf16[1024,256]{1,0:T(8,128)(2,1)} %hk_ref.1, bf16[1024,256]{1,0:T(8,128)(2,1)} %hv_ref.1, f32[1,128]{1,0:T(1,128)} %bitcast.3, f32[8,128]{1,0:T(8,128)} %bitcast.2, bf16[1024,256]{1,0:T(8,128)(2,1)} %hq_hbm.1, ...), custom_call_target="tpu_custom_call" | custom-call | tf_op jit(solution)/shard_map/pallas_call | solution.py:438
  79.0 3.4 %shard_map.132 = (bf16[1024,256]{1,0:T(8,128)(2,1)}, bf16[256,1024]{1,0:T(8,128)(2,1)}) custom-call(bf16[1024,256]{1,0:T(8,128)(2,1)} %get-tuple-element.4.banded_ref, bf16[256,1024]{1,0:T(8,128)(2,1)} %get-tuple-element.5.attended_ref), custom_call_target="tpu_custom_call" | custom-call | tf_op jit(solution)/shard_map/pallas_call | solution.py:408

commit v3 on v2

--- a/solution.py
+++ b/solution.py
@@ -70,10 +70,10 @@
     n,
     chans,
     order_ref,
-    hk_ref,
-    hv_ref,
     skip_ref,
     gain_ref,
+    hk_hbm,
+    hv_hbm,
     hq_hbm,
     filter_hbm,
     q_hbm,
@@ -83,6 +83,8 @@
     turns_hbm,
     banded_ref,
     attended_ref,
+    hk_ref,
+    hv_ref,
     gate_all,
     q_all,
     k_all,
@@ -152,11 +154,13 @@
         pl.semaphore_signal(barrier, inc=1, device_id={"chan": other}, device_id_type=MESH)
 
     staged = [
+        (hk_hbm, hk_ref),
+        (hv_hbm, hv_ref),
+        (hq_hbm, gate_all),
         (filter_hbm, filter_ref),
         (forward_hbm, forward_ref),
         (inverse_hbm, inverse_ref),
         (turns_hbm, turns_ref),
-        (hq_hbm, gate_all),
         (q_hbm, q_all),
         (k_hbm, k_all),
     ]
@@ -167,26 +171,30 @@
     for copy in staged:
         copy.start()
 
-    def make_product(index, unused):
-        part = pl.ds(pl.multiple_of(index * pencil, pencil), pencil)
-        product_out[index] = (
-            hk_ref[part, :].astype(jnp.float32) * hv_ref[part, :].astype(jnp.float32)
-        ).astype(jnp.bfloat16)
-        return unused
-
-    lax.fori_loop(0, n, make_product, 0)
-    pl.semaphore_wait(barrier, n - 1 + chans - 1)
-    staged[4].wait()
     products = exchange(PRODUCT, lambda d: product_out.at[d], product_in.at[me])
     queries = exchange(QUERIES, lambda d: column(q_all, d), q_in.at[me])
     keys = exchange(KEYS, lambda d: column(k_all, d), k_in.at[me])
     gates = exchange(GATES, lambda d: block(gate_all, d), gate_in.at[me])
-    for copy in products + gates:
+
+    def product_of(index):
+        return (
+            block(hk_ref, index)[...].astype(jnp.float32)
+            * block(hv_ref, index)[...].astype(jnp.float32)
+        ).astype(jnp.bfloat16)
+
+    staged[2].wait()
+    pl.semaphore_wait(barrier, n - 1 + chans - 1)
+    for copy in gates:
         copy.start()
-    product_in[me] = product_out[me]
+    for copy in staged[:2]:
+        copy.wait()
+    for offset in range(1, n):
+        product_out[peer(offset)] = product_of(peer(offset))
+        products[offset - 1].start()
+    product_in[me] = product_of(me)
     gate_in[me] = block(gate_all, me)[...]
 
-    for copy in staged[:4] + staged[5:]:
+    for copy in staged[3:]:
         copy.wait()
     q_in[me] = column(q_all, me)[...]
     k_in[me] = column(k_all, me)[...]
@@ -396,24 +404,6 @@
         copy.wait()
 
 
-def settle_kernel(banded_ref, attended_ref, banded_out, attended_out):
-    banded_out[...] = banded_ref[...]
-    attended_out[...] = attended_ref[...]
-
-
-def settled(*arrays):
-    specs = [
-        pl.BlockSpec((a.shape[0] // 4, a.shape[1]), lambda index: (index, 0)) for a in arrays
-    ]
-    return pl.pallas_call(
-        settle_kernel,
-        out_shape=tuple(jax.ShapeDtypeStruct(a.shape, a.dtype) for a in arrays),
-        grid=(4,),
-        in_specs=specs,
-        out_specs=specs,
-    )(*arrays)
-
-
 def fused(
     hyena_query,
     hyena_key,
@@ -431,19 +421,21 @@
     pencil = long_filter.shape[0]
     forward_table, inverse_table, turns = odd_tables(n, rows)
     vmem = pl.BlockSpec(memory_space=pltpu.VMEM)
-    anywhere = pl.BlockSpec(memory_space=pl.ANY)
+    far = pl.BlockSpec(memory_space=pl.ANY)
     bf16, f32 = jnp.bfloat16, jnp.float32
     wide = n * pencil
     tile = rows // TILES
-    outputs = pl.pallas_call(
+    return pl.pallas_call(
         functools.partial(fused_kernel, n, chans),
         out_shape=(
             jax.ShapeDtypeStruct((channels, rows), bf16),
             jax.ShapeDtypeStruct((rows, channels), bf16),
         ),
-        in_specs=[pl.BlockSpec(memory_space=pltpu.SMEM)] + [vmem] * 4 + [anywhere] * 7,
+        in_specs=[pl.BlockSpec(memory_space=pltpu.SMEM)] + [vmem] * 2 + [far] * 9,
         out_specs=(vmem, vmem),
         scratch_shapes=[
+            pltpu.VMEM((channels, rows), bf16),
+            pltpu.VMEM((channels, rows), bf16),
             pltpu.VMEM((channels, rows), bf16),
             pltpu.VMEM((rows, channels), bf16),
             pltpu.VMEM((rows, channels), bf16),
@@ -475,17 +467,17 @@
             pltpu.SemaphoreType.DMA((7, n)),
             pltpu.SemaphoreType.DMA((chans,)),
             pltpu.SemaphoreType.DMA((chans,)),
-            pltpu.SemaphoreType.DMA((7,)),
+            pltpu.SemaphoreType.DMA((9,)),
         ],
         compiler_params=pltpu.CompilerParams(
-            collective_id=0, has_side_effects=True, vmem_limit_bytes=56 * 1024 * 1024
+            collective_id=0, has_side_effects=True, vmem_limit_bytes=36 * 1024 * 1024
         ),
     )(
         stripe_order,
+        skip_weight.reshape(1, pencil),
+        norm_gain.reshape(n, pencil),
         hyena_key,
         hyena_value,
-        skip_weight.reshape(1, pencil),
-        norm_gain.reshape(n, pencil),
         hyena_query,
         long_filter,
         query_rows,
@@ -494,7 +486,6 @@
         jnp.asarray(inverse_table),
         jnp.asarray(turns),
     )
-    return settled(*outputs)
 
 
 def passed_along(block, axis, distance):

time: 82.6 us -> 93.9 us (1.14)
  the two profiles are of different devices: /device:TPU:0 before, /device:TPU:13 now
where the time goes in v3:
time: 93.9 us; the launch traced here: 93.3 us
  Pallas kernels  79.6 us (85%)
  local copies, waits for them, and re-layouts  13 us (14%)
    pallas_call x1, Pallas kernels, fused(): pl.pallas_call(functools.partial(fused_kernel, n, chans), out_shape=(jax....  79.6 us
    unnamed x26, local copies, waits for them, and re-layouts  13 us

profile of v3, /device:TPU:13, one launch (start us, length us, event | category | flops | bytes accessed | tf_op | source)
XLA Modules:
  0.0 93.3 jit_solution(6283523677292933596)
XLA Ops:
  0.6 0.0 copy-start.11
  0.6 0.6 copy-done.11
  1.3 0.0 copy-start
  1.3 1.2 %copy-done = f32[128,2048]{1,0:T(8,128)S(1)} copy-done((f32[128,2048]{1,0:T(8,128)S(1)}, f32[128,2048]{1,0:T(8,128)}, u32[]{:S(2)}) %copy-start) | copy-done | bytes 1048600
  2.5 0.0 copy-start.1
  2.5 1.0 %copy-done.1 = bf16[1024,256]{1,0:T(8,128)(2,1)S(1)} copy-done((bf16[1024,256]{1,0:T(8,128)(2,1)S(1)}, bf16[1024,256]{1,0:T(8,128)(2,1)}, u32[]{:S(2)}) %copy-start.1) | copy-done | bytes 524312
  3.6 0.0 copy-start.2
  3.6 1.0 %copy-done.2 = bf16[1024,256]{1,0:T(8,128)(2,1)S(1)} copy-done((bf16[1024,256]{1,0:T(8,128)(2,1)S(1)}, bf16[1024,256]{1,0:T(8,128)(2,1)}, u32[]{:S(2)}) %copy-start.2) | copy-done | bytes 524312
  4.6 0.0 copy-start.3
  4.6 1.0 %copy-done.3 = bf16[1024,256]{1,0:T(8,128)(2,1)S(1)} copy-done((bf16[1024,256]{1,0:T(8,128)(2,1)S(1)}, bf16[1024,256]{1,0:T(8,128)(2,1)}, u32[]{:S(2)}) %copy-start.3) | copy-done | bytes 524312
  5.6 0.0 copy-start.4
  5.6 1.0 %copy-done.4 = bf16[256,1024]{1,0:T(8,128)(2,1)S(1)} copy-done((bf16[256,1024]{1,0:T(8,128)(2,1)S(1)}, bf16[256,1024]{1,0:T(8,128)(2,1)}, u32[]{:S(2)}) %copy-start.4) | copy-done | bytes 524312
  6.7 0.0 copy-start.5
  6.7 1.0 %copy-done.5 = bf16[256,1024]{1,0:T(8,128)(2,1)S(1)} copy-done((bf16[256,1024]{1,0:T(8,128)(2,1)S(1)}, bf16[256,1024]{1,0:T(8,128)(2,1)}, u32[]{:S(2)}) %copy-start.5) | copy-done | bytes 524312
  7.7 0.0 copy-start.6
  7.7 1.0 %copy-done.6 = bf16[2,256,512]{2,1,0:T(8,128)(2,1)S(1)} copy-done((bf16[2,256,512]{2,1,0:T(8,128)(2,1)S(1)}, bf16[2,256,512]{2,1,0:T(8,128)(2,1)}, u32[]{:S(2)}) %copy-start.6) | copy-done | bytes 524312
  8.8 0.0 copy-start.7
  8.8 1.0 %copy-done.7 = bf16[2,512,256]{2,1,0:T(8,128)(2,1)S(1)} copy-done((bf16[2,512,256]{2,1,0:T(8,128)(2,1)S(1)}, bf16[2,512,256]{2,1,0:T(8,128)(2,1)}, u32[]{:S(2)}) %copy-start.7) | copy-done | bytes 524312
  9.8 0.0 copy-start.8
  9.8 0.9 copy-done.8
  10.7 0.0 copy-start.9
  10.7 0.7 copy-done.9
  11.4 0.0 copy-start.10
  11.4 0.7 copy-done.10
  12.1 79.6 %shard_map.131 = (bf16[1024,256]{1,0:T(8,128)(2,1)S(1)}, bf16[256,1024]{1,0:T(8,128)(2,1)S(1)}) custom-call(s32[2048]{0:T(1024)S(1)} %copy-done.9, f32[1,128]{1,0:T(1,128)S(1)} %bitcast.3, f32[8,128]{1,0:T(8,128)S(1)} %bitcast.2, bf16[1024,256]{1,0:T(8,128)(2,1)S(1)} %copy-done.1, bf16[1024,256]{1,0:T(8,128)(2,1)S(1)} %copy-done.2, ...), custom_call_target="tpu_custom_call" | custom-call | tf_op jit(solution)/shard_map/pallas_call | solution.py:428
  91.7 0.8 copy.16
  92.5 0.8 copy.17
Async XLA Ops:
  0.6 0.7 copy-start.11
  1.3 1.2 %copy-start = (f32[128,2048]{1,0:T(8,128)S(1)}, f32[128,2048]{1,0:T(8,128)}, u32[]{:S(2)}) copy-start(f32[128,2048]{1,0:T(8,128)} %filter_hbm.1) | copy-start | bytes 3145732
  2.5 1.0 %copy-start.1 = (bf16[1024,256]{1,0:T(8,128)(2,1)S(1)}, bf16[1024,256]{1,0:T(8,128)(2,1)}, u32[]{:S(2)}) copy-start(bf16[1024,256]{1,0:T(8,128)(2,1)} %hk_hbm.1) | copy-start | bytes 1572868
  3.6 1.0 %copy-start.2 = (bf16[1024,256]{1,0:T(8,128)(2,1)S(1)}, bf16[1024,256]{1,0:T(8,128)(2,1)}, u32[]{:S(2)}) copy-start(bf16[1024,256]{1,0:T(8,128)(2,1)} %hv_hbm.1) | copy-start | bytes 1572868
  4.6 1.0 %copy-start.3 = (bf16[1024,256]{1,0:T(8,128)(2,1)S(1)}, bf16[1024,256]{1,0:T(8,128)(2,1)}, u32[]{:S(2)}) copy-start(bf16[1024,256]{1,0:T(8,128)(2,1)} %hq_hbm.1) | copy-start | bytes 1572868
  5.6 1.0 %copy-start.4 = (bf16[256,1024]{1,0:T(8,128)(2,1)S(1)}, bf16[256,1024]{1,0:T(8,128)(2,1)}, u32[]{:S(2)}) copy-start(bf16[256,1024]{1,0:T(8,128)(2,1)} %q_hbm.1) | copy-start | bytes 1572868
  6.7 1.0 %copy-start.5 = (bf16[256,1024]{1,0:T(8,128)(2,1)S(1)}, bf16[256,1024]{1,0:T(8,128)(2,1)}, u32[]{:S(2)}) copy-start(bf16[256,1024]{1,0:T(8,128)(2,1)} %k_hbm.1) | copy-start | bytes 1572868
  7.7 1.0 %copy-start.6 = (bf16[2,256,512]{2,1,0:T(8,128)(2,1)S(1)}, bf16[2,256,512]{2,1,0:T(8,128)(2,1)}, u32[]{:S(2)}) copy-start(bf16[2,256,512]{2,1,0:T(8,128)(2,1)} %constant.7.clone.inverse_hbm) | copy-start | bytes 1572868
  8.8 1.0 %copy-start.7 = (bf16[2,512,256]{2,1,0:T(8,128)(2,1)S(1)}, bf16[2,512,256]{2,1,0:T(8,128)(2,1)}, u32[]{:S(2)}) copy-start(bf16[2,512,256]{2,1,0:T(8,128)(2,1)} %constant.6.clone.forward_hbm) | copy-start | bytes 1572868
  9.8 0.9 copy-start.8
  10.7 0.7 copy-start.9
  11.4 0.7 copy-start.10

commit v4 on v3

--- a/solution.py
+++ b/solution.py
@@ -127,23 +127,38 @@
     def peer(offset):
         return lax.rem(me + offset, n)
 
+    half = n // 2
+    inner = lax.rem(me, half)
+    near, across = me - inner, half - (me - inner)
+    phase = lax.rem(my_chan + me // 2, 2)
+    targets = []
+    for turn in range(half):
+        far = across + lax.rem(inner + turn, half)
+        if turn == half - 1:
+            targets.append(far)
+        else:
+            beside = near + lax.rem(inner + 1 + turn, half)
+            targets.append(far * (1 - phase) + beside * phase)
+            targets.append(beside * (1 - phase) + far * phase)
+    offsets = [lax.rem(target - me + n, n) for target in targets]
+
     def block(ref, index):
         return ref.at[pl.ds(pl.multiple_of(index * pencil, pencil), pencil), :]
 
     def column(ref, index):
         return ref.at[:, pl.ds(pl.multiple_of(index * pencil, pencil), pencil)]
 
-    def exchange(kind, source, target):
+    def exchange(kind, source, here):
         return [
             pltpu.make_async_remote_copy(
-                src_ref=source(peer(offset)),
-                dst_ref=target,
+                src_ref=source(target),
+                dst_ref=here,
                 send_sem=send_sem.at[kind, offset],
                 recv_sem=recv_sem.at[kind, offset],
-                device_id={"seq": peer(offset)},
+                device_id={"seq": target},
                 device_id_type=MESH,
             )
-            for offset in range(1, n)
+            for target, offset in zip(targets, offsets)
         ]
 
     barrier = pltpu.get_barrier_semaphore()
@@ -182,15 +197,15 @@
             * block(hv_ref, index)[...].astype(jnp.float32)
         ).astype(jnp.bfloat16)
 
+    for copy in staged[:2]:
+        copy.wait()
+    pl.semaphore_wait(barrier, n - 1 + chans - 1)
+    for target, copy in zip(targets, products):
+        product_out[target] = product_of(target)
+        copy.start()
     staged[2].wait()
-    pl.semaphore_wait(barrier, n - 1 + chans - 1)
     for copy in gates:
         copy.start()
-    for copy in staged[:2]:
-        copy.wait()
-    for offset in range(1, n):
-        product_out[peer(offset)] = product_of(peer(offset))
-        products[offset - 1].start()
     product_in[me] = product_of(me)
     gate_in[me] = block(gate_all, me)[...]
 
@@ -268,9 +283,6 @@
     for copy in products:
         copy.wait()
 
-    for copy in keys:
-        copy.start()
-
     def stand_up(source):
         for s in range(n):
             upright[s * rows : (s + 1) * rows, :] = source[s].astype(jnp.float32).T
@@ -302,10 +314,6 @@
 
     banded = exchange(BANDED, lambda d: gated_out.at[d], block(banded_ref, me))
     ones = jnp.ones((8, pencil), jnp.float32)
-    for offset in list(range(1, n)) + [0]:
-        to = peer(offset)
-        mine = gated[order_ref[to * rows]].astype(jnp.float32)
-        gated_out[to] = mine.T.astype(jnp.bfloat16)
     for s in range(n):
         mine = gated[order_ref[s * rows]].astype(jnp.float32)
         values[s] = mine.astype(jnp.bfloat16)
@@ -316,7 +324,7 @@
             precision=lax.Precision.HIGHEST,
             preferred_element_type=jnp.float32,
         )[:1]
-    across = [
+    beside_chan = [
         pltpu.make_async_remote_copy(
             src_ref=squares,
             dst_ref=squares_chan.at[offset],
@@ -327,9 +335,9 @@
         )
         for offset in range(1, chans)
     ]
-    for copy in across:
+    for copy in beside_chan:
         copy.start()
-    for copy in across:
+    for copy in beside_chan:
         copy.wait()
     squares_sum[...] = functools.reduce(
         jnp.add, [squares[...]] + [squares_chan[offset] for offset in range(1, chans)]
@@ -337,6 +345,10 @@
     along = exchange(SQUARES, lambda d: squares_sum, squares_seq.at[me])
     for copy in along:
         copy.start()
+    for copy in keys:
+        copy.start()
+    for s in range(n):
+        gated_out[s] = gated[order_ref[s * rows]].astype(jnp.float32).T.astype(jnp.bfloat16)
     squares_seq[me] = squares_sum[...]
     for copy in along:
         copy.wait()
@@ -359,7 +371,6 @@
         copy.wait_recv()
 
     factor = math.log2(math.e) / math.sqrt(HEAD_DIM)
-    half = n // 2
     height = half * tile
     attended = exchange(ATTENDED, lambda d: result.at[d], column(attended_ref, me))
 
@@ -390,11 +401,11 @@
             result[pl.ds(first, half), jt * tile : (jt + 1) * tile, :] = part.reshape(
                 half, tile, pencil
             )
-        for offset in range(1, n):
-
-            @pl.when(peer(offset) // half == h)
+        for target, copy in zip(targets, attended):
+
+            @pl.when(target // half == h)
             def send():
-                attended[offset - 1].start()
+                copy.start()
 
         return unused
 
@@ -470,7 +481,7 @@
             pltpu.SemaphoreType.DMA((9,)),
         ],
         compiler_params=pltpu.CompilerParams(
-            collective_id=0, has_side_effects=True, vmem_limit_bytes=36 * 1024 * 1024
+            collective_id=0, has_side_effects=True, vmem_limit_bytes=60 * 1024 * 1024
         ),
     )(
         stripe_order,

time: 93.9 us -> 84.3 us (0.90)
  the two profiles are of different devices: /device:TPU:13 before, /device:TPU:0 now
where the time goes in v4:
time: 84.3 us; the launch traced here: 84.1 us
  Pallas kernels  80.7 us (96%)
  local copies, waits for them, and re-layouts  2.72 us (3%)
    pallas_call x1, Pallas kernels, fused(): pl.pallas_call(functools.partial(fused_kernel, n, chans), out_shape=(jax....  80.7 us
    unnamed x4, local copies, waits for them, and re-layouts  2.72 us

profile of v4, /device:TPU:0, one launch (start us, length us, event | category | flops | bytes accessed | tf_op | source)
XLA Modules:
  0.0 84.1 jit_solution(1541381528661898023)
XLA Ops:
  0.6 80.7 %shard_map.131 = (bf16[1024,256]{1,0:T(8,128)(2,1)}, bf16[256,1024]{1,0:T(8,128)(2,1)}) custom-call(s32[2048]{0:T(1024)} %order_ref.1, f32[1,128]{1,0:T(1,128)} %bitcast.3, f32[8,128]{1,0:T(8,128)} %bitcast.2, bf16[1024,256]{1,0:T(8,128)(2,1)} %hk_hbm.1, bf16[1024,256]{1,0:T(8,128)(2,1)} %hv_hbm.1, bf16[1024,256]{1,0:T(8,128)(2,1)} %hq_hbm.1, ...), custom_call_target="tpu_custom_call" | custom-call | tf_op jit(solution)/shard_map/pallas_call | solution.py:439
  81.4 0.0 copy-start
  81.4 1.9 %copy.16 = bf16[1024,256]{1,0:T(8,128)(2,1)} copy(bf16[1024,256]{1,0:T(8,128)(2,1)} %get-tuple-element.4) | data formatting | bytes 1048576
  83.3 0.0 copy-done
  83.3 0.8 copy.17
Async XLA Ops:
  81.4 1.9 %copy-start = (bf16[256,1024]{1,0:T(8,128)(2,1)S(1)}, bf16[256,1024]{1,0:T(8,128)(2,1)}, u32[]{:S(2)}) copy-start(bf16[256,1024]{1,0:T(8,128)(2,1)} %get-tuple-element.5) | copy-start | bytes 1572868

commit v5 on v4

--- a/solution.py
+++ b/solution.py
@@ -15,7 +15,6 @@
 TILES = 4
 MESH = pl.DeviceIdType.MESH
 PRODUCT, QUERIES, KEYS, GATES, BANDED, ATTENDED, SQUARES = range(7)
-TRANSPOSED = (((1,), (1,)), ((), ()))
 
 
 def high_low(table):
@@ -112,6 +111,7 @@
     squares_sum,
     squares_seq,
     bias,
+    turned_keys,
     send_sem,
     recv_sem,
     chan_send,
@@ -269,23 +269,26 @@
     for copy in queries:
         copy.start()
 
-    def place_of(index, count):
-        inner = lax.rem(index, tile)
-        place = n * inner
-        for s in range(n):
-            place = place + jnp.where(index // tile == s, order_ref[s * rows], 0)
+    def place_of(index):
+        place = n * index + order_ref[0]
+        for s in range(1, n):
+            change = order_ref[s * rows] - order_ref[(s - 1) * rows] - n * tile
+            place = place + jnp.where(index >= s * tile, change, 0)
         return place
 
-    key_place = place_of(lax.broadcasted_iota(jnp.int32, (8, wide_tile), 1), wide_tile)[:1]
-    query_place = place_of(lax.broadcasted_iota(jnp.int32, (wide_tile, 128), 0), wide_tile)[:, :1]
+    key_place = place_of(lax.broadcasted_iota(jnp.int32, (8, wide_tile), 1))[:1]
+    query_place = place_of(lax.broadcasted_iota(jnp.int32, (wide_tile, 128), 0))[:, :1]
     bias[...] = jnp.where(key_place <= query_place, 0.0, -1e30)
 
     for copy in products:
         copy.wait()
 
+    for copy in keys:
+        copy.start()
+
     def stand_up(source):
         for s in range(n):
-            upright[s * rows : (s + 1) * rows, :] = source[s].astype(jnp.float32).T
+            upright[s * rows : (s + 1) * rows, :] = source[s].T.astype(jnp.float32)
 
     stand_up(product_in)
     for t in range(0, n, 2):
@@ -313,17 +316,16 @@
         gated[t] = (upright[pl.ds(t, rows, stride=n), :] * convolved[t]).astype(jnp.bfloat16)
 
     banded = exchange(BANDED, lambda d: gated_out.at[d], block(banded_ref, me))
-    ones = jnp.ones((8, pencil), jnp.float32)
+    lane = lax.broadcasted_iota(jnp.int32, (pencil, pencil), 1)
+    summed_squares = jnp.zeros((rows, pencil), jnp.float32)
     for s in range(n):
-        mine = gated[order_ref[s * rows]].astype(jnp.float32)
-        values[s] = mine.astype(jnp.bfloat16)
-        squares[s : s + 1, :] = lax.dot_general(
-            ones,
-            mine * mine,
-            TRANSPOSED,
-            precision=lax.Precision.HIGHEST,
-            preferred_element_type=jnp.float32,
-        )[:1]
+        mine = gated[order_ref[s * rows]]
+        values[s] = mine
+        wide = mine.astype(jnp.float32)
+        high, low = split(wide * wide)
+        pick = jnp.where(lane == s, 1.0, 0.0).astype(jnp.bfloat16)
+        summed_squares = summed_squares + dot(high, pick) + dot(low, pick)
+    squares[...] = summed_squares.T[:n, :]
     beside_chan = [
         pltpu.make_async_remote_copy(
             src_ref=squares,
@@ -345,21 +347,9 @@
     along = exchange(SQUARES, lambda d: squares_sum, squares_seq.at[me])
     for copy in along:
         copy.start()
-    for copy in keys:
-        copy.start()
     for s in range(n):
-        gated_out[s] = gated[order_ref[s * rows]].astype(jnp.float32).T.astype(jnp.bfloat16)
+        gated_out[s] = values[s].T
     squares_seq[me] = squares_sum[...]
-    for copy in along:
-        copy.wait()
-    inverse_rms = lax.rsqrt(
-        functools.reduce(jnp.add, [squares_seq[s] for s in range(n)]) / D + 1e-05
-    )
-    gain = gain_ref[pl.ds(me, 1), :]
-    for s in range(n):
-        scale = jnp.broadcast_to(inverse_rms[s : s + 1, :], (pencil, rows)).T
-        values[s] = (values[s].astype(jnp.float32) * scale * gain).astype(jnp.bfloat16)
-
     for copy in keys:
         copy.wait_send()
     for copy in banded:
@@ -369,6 +359,20 @@
         copy.wait()
     for copy in keys:
         copy.wait_recv()
+    for kt in range(TILES):
+        key = k_in[:, kt * tile : (kt + 1) * tile, :].reshape(wide_tile, pencil)
+        turned_keys[kt] = key.T
+    for copy in along:
+        copy.wait()
+    inverse_rms = lax.rsqrt(
+        functools.reduce(jnp.add, [squares_seq[s] for s in range(n)]) / D + 1e-05
+    )
+    gain = gain_ref[pl.ds(me, 1), :]
+    scales = jnp.concatenate([inverse_rms] * (pencil // n), axis=0).T
+    for s in range(n):
+        values[s] = (values[s].astype(jnp.float32) * scales[:, s : s + 1] * gain).astype(
+            jnp.bfloat16
+        )
 
     factor = math.log2(math.e) / math.sqrt(HEAD_DIM)
     height = half * tile
@@ -382,10 +386,7 @@
             query = query.reshape(height, pencil)
             scores = []
             for kt in range(jt + 1):
-                key = k_in[:, kt * tile : (kt + 1) * tile, :].reshape(wide_tile, pencil)
-                score = lax.dot_general(
-                    query, key, TRANSPOSED, preferred_element_type=jnp.float32
-                )
+                score = dot(query, turned_keys[kt])
                 if kt == jt:
                     score = score + bias[pl.ds(pl.multiple_of(h * height, height), height), :]
                 scores.append(score)
@@ -474,6 +475,7 @@
             pltpu.VMEM((n, rows), f32),
             pltpu.VMEM((n, n, rows), f32),
             pltpu.VMEM((n * tile, n * tile), f32),
+            pltpu.VMEM((TILES, pencil, n * tile), bf16),
             pltpu.SemaphoreType.DMA((7, n)),
             pltpu.SemaphoreType.DMA((7, n)),
             pltpu.SemaphoreType.DMA((chans,)),

time: 84.3 us -> 83 us (0.985)
  Pallas kernels: 80.7 us -> 79.4 us
    pallas_call x1, Pallas kernels: 80.7 us -> 79.4 us  [fused(): pl.pallas_call(functools.partial(fused_kernel, n, chans), out_shape=(jax....]
where the time goes in v5:
time: 83 us; the launch traced here: 82.8 us
  Pallas kernels  79.4 us (96%)
  local copies, waits for them, and re-layouts  2.72 us (3%)
    pallas_call x1, Pallas kernels, fused(): pl.pallas_call(functools.partial(fused_kernel, n, chans), out_shape=(jax....  79.4 us
    unnamed x4, local copies, waits for them, and re-layouts  2.72 us

profile of v5, /device:TPU:0, one launch (start us, length us, event | category | flops | bytes accessed | tf_op | source)
XLA Modules:
  0.0 82.8 jit_solution(8187503818693899506)
XLA Ops:
  0.6 79.4 %shard_map.131 = (bf16[1024,256]{1,0:T(8,128)(2,1)}, bf16[256,1024]{1,0:T(8,128)(2,1)}) custom-call(s32[2048]{0:T(1024)} %order_ref.1, f32[1,128]{1,0:T(1,128)} %bitcast.3, f32[8,128]{1,0:T(8,128)} %bitcast.2, bf16[1024,256]{1,0:T(8,128)(2,1)} %hk_hbm.1, bf16[1024,256]{1,0:T(8,128)(2,1)} %hv_hbm.1, bf16[1024,256]{1,0:T(8,128)(2,1)} %hq_hbm.1, ...), custom_call_target="tpu_custom_call" | custom-call | tf_op jit(solution)/shard_map/pallas_call | solution.py:440
  80.0 0.0 copy-start
  80.0 1.9 %copy.16 = bf16[1024,256]{1,0:T(8,128)(2,1)} copy(bf16[1024,256]{1,0:T(8,128)(2,1)} %get-tuple-element.4) | data formatting | bytes 1048576
  82.0 0.0 copy-done
  82.0 0.8 copy.17
Async XLA Ops:
  80.0 1.9 %copy-start = (bf16[256,1024]{1,0:T(8,128)(2,1)S(1)}, bf16[256,1024]{1,0:T(8,128)(2,1)}, u32[]{:S(2)}) copy-start(bf16[256,1024]{1,0:T(8,128)(2,1)} %get-tuple-element.5) | copy-start | bytes 1572868

commit v6 on v5

--- a/solution.py
+++ b/solution.py
@@ -28,9 +28,8 @@
     angle = 2.0 * np.pi * frequency[:, None] * np.arange(rows)[None, :] / (2 * rows)
     dense = np.concatenate((np.cos(angle), -np.sin(angle)), axis=0)
     twist = 2.0 * np.pi * frequency[:, None] * np.arange(stripes)[None, :] / (2 * rows * stripes)
-    turns = np.zeros((rows, 128), np.float32)
-    turns[:, :stripes] = np.cos(twist)
-    turns[:, stripes : 2 * stripes] = np.sin(twist)
+    turns = np.stack((np.cos(twist), np.sin(twist))).astype(np.float32)
+    turns = np.repeat(turns, HEAD_DIM, axis=2)
     return high_low(dense), high_low(dense.T), turns
 
 
@@ -215,13 +214,13 @@
     k_in[me] = column(k_all, me)[...]
 
     def turned_sections(part):
-        cos = turns_ref[part, :]
         parts = []
         for t in range(n):
             real = section[part, t * pencil : (t + 1) * pencil]
             below = pl.ds(pl.multiple_of(rows + part.start, part.size), part.size)
             imag = section[below, t * pencil : (t + 1) * pencil]
-            c, s = cos[:, t : t + 1], cos[:, n + t : n + t + 1]
+            lanes = slice(t * pencil, (t + 1) * pencil)
+            c, s = turns_ref[0, part, lanes], turns_ref[1, part, lanes]
             parts.append((real * c + imag * s, imag * c - real * s))
         return small_dft(parts, -1.0)
 
@@ -245,10 +244,9 @@
             parts.append(
                 (real * other_real - imag * other_imag, real * other_imag + imag * other_real)
             )
-        cos = turns_ref[part, :]
         for t, (real, imag) in enumerate(small_dft(parts, 1.0)):
-            c, s = cos[:, t : t + 1], cos[:, n + t : n + t + 1]
             lanes = slice(t * pencil, (t + 1) * pencil)
+            c, s = turns_ref[0, part, lanes], turns_ref[1, part, lanes]
             for place, value in ((part, real * c - imag * s), (below, real * s + imag * c)):
                 high, low = split(value)
                 back[0, place, lanes] = high
@@ -320,7 +318,7 @@
     summed_squares = jnp.zeros((rows, pencil), jnp.float32)
     for s in range(n):
         mine = gated[order_ref[s * rows]]
-        values[s] = mine
+        values[s] = jnp.concatenate((mine, jnp.ones_like(mine)), axis=1)
         wide = mine.astype(jnp.float32)
         high, low = split(wide * wide)
         pick = jnp.where(lane == s, 1.0, 0.0).astype(jnp.bfloat16)
@@ -348,7 +346,7 @@
     for copy in along:
         copy.start()
     for s in range(n):
-        gated_out[s] = values[s].T
+        gated_out[s] = values[s, :, :pencil].T
     squares_seq[me] = squares_sum[...]
     for copy in keys:
         copy.wait_send()
@@ -370,9 +368,8 @@
     gain = gain_ref[pl.ds(me, 1), :]
     scales = jnp.concatenate([inverse_rms] * (pencil // n), axis=0).T
     for s in range(n):
-        values[s] = (values[s].astype(jnp.float32) * scales[:, s : s + 1] * gain).astype(
-            jnp.bfloat16
-        )
+        normed = values[s, :, :pencil].astype(jnp.float32) * scales[:, s : s + 1] * gain
+        values[s, :, :pencil] = normed.astype(jnp.bfloat16)
 
     factor = math.log2(math.e) / math.sqrt(HEAD_DIM)
     height = half * tile
@@ -390,15 +387,13 @@
                 if kt == jt:
                     score = score + bias[pl.ds(pl.multiple_of(h * height, height), height), :]
                 scores.append(score)
-            top = functools.reduce(jnp.maximum, [jnp.max(s, axis=1, keepdims=True) for s in scores])
-            total = jnp.zeros((height, 1), jnp.float32)
-            summed = jnp.zeros((height, pencil), jnp.float32)
+            top = jnp.max(functools.reduce(jnp.maximum, scores), axis=1, keepdims=True)
+            summed = jnp.zeros((height, 2 * pencil), jnp.float32)
             for kt, score in enumerate(scores):
                 weight = jnp.exp2((score - top) * factor)
-                total = total + jnp.sum(weight, axis=1, keepdims=True)
-                value = values[:, kt * tile : (kt + 1) * tile, :].reshape(wide_tile, pencil)
+                value = values[:, kt * tile : (kt + 1) * tile, :].reshape(wide_tile, 2 * pencil)
                 summed = summed + dot(weight.astype(jnp.bfloat16), value)
-            part = (summed / total).astype(jnp.bfloat16)
+            part = (summed[:, :pencil] / summed[:, pencil:]).astype(jnp.bfloat16)
             result[pl.ds(first, half), jt * tile : (jt + 1) * tile, :] = part.reshape(
                 half, tile, pencil
             )
@@ -468,7 +463,7 @@
             pltpu.VMEM((n, rows, pencil), f32),
             pltpu.VMEM((n, rows, pencil), bf16),
             pltpu.VMEM((n, pencil, rows), bf16),
-            pltpu.VMEM((n, rows, pencil), bf16),
+            pltpu.VMEM((n, rows, 2 * pencil), bf16),
             pltpu.VMEM((n, rows, pencil), bf16),
             pltpu.VMEM((n, rows), f32),
             pltpu.VMEM((chans, n, rows), f32),

time: 83 us -> 84 us (1.012)
  local copies, waits for them, and re-layouts: 2.72 us -> 3.74 us
    unnamed x4 -> x2, local copies, waits for them, and re-layouts: 2.72 us -> 3.74 us
where the time goes in v6:
time: 84 us; the launch traced here: 83.8 us
  Pallas kernels  79.4 us (95%)
  local copies, waits for them, and re-layouts  3.74 us (4%)
    pallas_call x1, Pallas kernels, fused(): pl.pallas_call(functools.partial(fused_kernel, n, chans), out_shape=(jax....  79.4 us
    unnamed x2, local copies, waits for them, and re-layouts  3.74 us

profile of v6, /device:TPU:0, one launch (start us, length us, event | category | flops | bytes accessed | tf_op | source)
XLA Modules:
  0.0 83.8 jit_solution(16665910982002563275)
XLA Ops:
  0.6 79.4 %shard_map.131 = (bf16[1024,256]{1,0:T(8,128)(2,1)}, bf16[256,1024]{1,0:T(8,128)(2,1)}) custom-call(s32[2048]{0:T(1024)} %order_ref.1, f32[1,128]{1,0:T(1,128)} %bitcast.3, f32[8,128]{1,0:T(8,128)} %bitcast.2, bf16[1024,256]{1,0:T(8,128)(2,1)} %hk_hbm.1, bf16[1024,256]{1,0:T(8,128)(2,1)} %hv_hbm.1, bf16[1024,256]{1,0:T(8,128)(2,1)} %hq_hbm.1, ...), custom_call_target="tpu_custom_call" | custom-call | tf_op jit(solution)/shard_map/pallas_call | solution.py:435
  80.0 1.9 %copy.16 = bf16[1024,256]{1,0:T(8,128)(2,1)} copy(bf16[1024,256]{1,0:T(8,128)(2,1)} %get-tuple-element.4) | data formatting | bytes 1048576
  81.9 1.9 %copy.17 = bf16[256,1024]{1,0:T(8,128)(2,1)} copy(bf16[256,1024]{1,0:T(8,128)(2,1)} %get-tuple-element.5) | data formatting | bytes 1048576
